TPU v7x, 32 devices: a whole 2x2x4 slice. The times are simulated.
32 devices in a mesh: row: 8 (over y, x, core), col: 4 (over z).
Axes of the slice: x: 2, y: 2, z: 4, core: 2. Of those that a mesh axis runs over, the one named last changes fastest.
Arguments:
- vectors: float32 [96, 65536], P(None, ('col', 'row')), may hold values from -6 to 6
- blocks: float32 [8, 4, 176, 128, 128], P('row', 'col'), may hold values from -0.15625 to 0.15625
- block_row: int32 [8, 4, 176], P('row', 'col'), may hold values from 0 to 63
- block_col: int32 [8, 4, 176], P('row', 'col'), may hold values from 0 to 127
- block_count: int32 [8, 4], P('row', 'col'), may hold values from 22 to 176, as said below
- lower_bound: float32 [1], replicated, may hold values from -2.5 to -1.5
- upper_bound: float32 [1], replicated, may hold values from 1.5 to 2.5
Outputs:
- filtered: float32 [96, 65536], P(None, ('col', 'row'))
Inputs may be any that keep to these rules, and one draw needn't show every extreme that they name: `block_row`: local block row index within the device's band. `block_col`: local block column index within the device's band. `block_count`: in every row of the device grid one device has all 176 slots stored.
All inputs are finite; a program needn't handle non-finite values.
Results may differ from a plain program's by a relative error of at most 0.0003.
Values sent between devices are 32-bit elements; how exact they have to be, the bound alone decides.
A program may use at most 128 MiB of HBM per device.

v0:
```python
import jax
import jax.numpy as jnp
from jax import lax
from jax.sharding import PartitionSpec as P

BS = 128


def local_products(col_tile, row_tile, device_blocks, rows_local, cols_local, live_mask):
    vector_count = col_tile.shape[0]
    col_blocks = col_tile.shape[1] // BS
    row_blocks = row_tile.shape[1] // BS
    col_view = col_tile.reshape(vector_count, col_blocks, BS)
    row_view = row_tile.reshape(vector_count, row_blocks, BS)
    source_col = jnp.take(col_view, cols_local, axis=1)
    forward = jnp.einsum("sij,vsj->vsi", device_blocks, source_col, precision=lax.Precision.HIGHEST)
    source_row = jnp.take(row_view, rows_local, axis=1)
    backward = jnp.einsum(
        "sij,vsi->vsj", device_blocks, source_row, precision=lax.Precision.HIGHEST
    )
    row_onehot = (jnp.arange(row_blocks)[:, None] == rows_local[None, :]).astype(
        jnp.float32
    ) * live_mask[None, :]
    col_onehot = (jnp.arange(col_blocks)[:, None] == cols_local[None, :]).astype(
        jnp.float32
    ) * live_mask[None, :]
    forward_part = jnp.einsum("rs,vsi->vri", row_onehot, forward, precision=lax.Precision.HIGHEST)
    backward_part = jnp.einsum("cs,vsj->vcj", col_onehot, backward, precision=lax.Precision.HIGHEST)
    return (forward_part.reshape(vector_count, -1), backward_part.reshape(vector_count, -1))


def mirrored_tile(vectors, row_index, col_count, row_ratio):
    vector_count, piece_size = vectors.shape
    sub_width = piece_size // col_count
    items = jnp.transpose(vectors.reshape(vector_count, col_count, sub_width), (1, 0, 2))
    arrived = lax.all_to_all(items, "col", split_axis=0, concat_axis=0, tiled=True)
    ratio_mask = (jnp.arange(row_ratio) == row_index // col_count).astype(jnp.float32)
    slots = arrived[:, None] * ratio_mask[None, :, None, None]
    slots = slots.reshape(col_count * row_ratio, vector_count, sub_width)
    dealt = lax.all_to_all(slots, "row", split_axis=0, concat_axis=0, tiled=True)
    mine = lax.dynamic_slice_in_dim(dealt, row_index % row_ratio * col_count, col_count, 0)
    whole = lax.all_gather(mine[None], "col", axis=0, tiled=True)
    return jnp.transpose(whole, (2, 1, 0, 3)).reshape(vector_count, col_count * piece_size)


def mirrored_sums(forward_part, row_index, col_count, row_ratio, piece_size):
    vector_count = forward_part.shape[0]
    sub_width = piece_size // col_count
    arranged = jnp.transpose(
        forward_part.reshape(vector_count, col_count, col_count, sub_width), (2, 1, 0, 3)
    )
    shared = lax.psum_scatter(arranged, "col", scatter_dimension=0, tiled=True)[0]
    ratio_mask = (jnp.arange(row_ratio) == row_index % row_ratio).astype(jnp.float32)
    slots = (ratio_mask[:, None, None, None] * shared[None]).reshape(
        row_ratio * col_count, vector_count, sub_width
    )
    dealt = lax.all_to_all(slots, "row", split_axis=0, concat_axis=0, tiled=True)
    picked = lax.dynamic_index_in_dim(
        dealt.reshape(col_count, row_ratio, vector_count, sub_width),
        row_index // col_count,
        1,
        keepdims=False,
    )
    returned = lax.all_to_all(picked, "col", split_axis=0, concat_axis=0, tiled=True)
    return jnp.transpose(returned, (1, 0, 2)).reshape(vector_count, piece_size)


def apply_hamiltonian(vectors, device_blocks, rows_local, cols_local, live_mask):
    col_tile = lax.all_gather(vectors, "row", axis=1, tiled=True)
    row_index = lax.axis_index("row")
    col_count = lax.axis_size("col")
    row_ratio = lax.axis_size("row") // col_count
    piece_size = vectors.shape[1]
    row_tile = mirrored_tile(vectors, row_index, col_count, row_ratio)
    forward_part, backward_part = local_products(
        col_tile, row_tile, device_blocks, rows_local, cols_local, live_mask
    )
    own_rows = mirrored_sums(forward_part, row_index, col_count, row_ratio, piece_size)
    return lax.psum_scatter(backward_part, "row", scatter_dimension=1, tiled=True) + own_rows


def body(vectors, blocks, block_row, block_col, block_count, lower_bound, upper_bound):
    device_blocks = blocks[0, 0]
    rows_local = block_row[0, 0]
    cols_local = block_col[0, 0]
    live_mask = (jnp.arange(device_blocks.shape[0]) < block_count[0, 0]).astype(jnp.float32)
    center = (upper_bound[0] + lower_bound[0]) / 2.0
    half_width = (upper_bound[0] - lower_bound[0]) / 2.0
    previous = vectors
    product = apply_hamiltonian(vectors, device_blocks, rows_local, cols_local, live_mask)
    current = (product - center * vectors) / half_width
    product = apply_hamiltonian(current, device_blocks, rows_local, cols_local, live_mask)
    following = 2.0 * (product - center * current) / half_width - previous
    previous, current = (current, following)
    return current


def solution(mesh):
    placed = (
        P(None, ("col", "row")),
        P("row", "col", None, None, None),
        P("row", "col", None),
        P("row", "col", None),
        P("row", "col"),
        P(),
        P(),
    )
    return jax.shard_map(
        body, mesh=mesh, in_specs=placed, out_specs=P(None, ("col", "row")), check_vma=False
    )
```

profile of v0, /device:TPU:0, one launch (start us, length us, event | category | flops | bytes accessed | tf_op | source)
XLA Modules:
  0.0 547.5 jit_solution(7364342070947036131)
XLA Ops:
  16.5 20.0 %all-to-all-done = f32[4,96,512]{2,1,0:T(8,128)S(1)} async-done(((f32[4,96,512]{2,1,0:T(8,128)}), f32[4,96,512]{2,1,0:T(8,128)S(1)}, u32[]{:S(2)}, u32[]{:S(2)}) %all-to-all-start) | async-done | bytes 786464 | tf_op jit(solution)/shard_map/all_to_all | solution.py:36
  41.7 31.7 %all-to-all-done.1 = f32[8,96,512]{2,1,0:T(8,128)S(1)} async-done(((f32[8,96,512]{2,1,0:T(8,128)}), f32[8,96,512]{2,1,0:T(8,128)S(1)}, u32[]{:S(2)}, u32[]{:S(2)}) %all-to-all-start.1) | async-done | bytes 1572896 | tf_op jit(solution)/shard_map/all_to_all | solution.py:40
  81.5 7.7 %gather_fusion.1 = f32[176,96,128]{2,1,0:T(8,128)} fusion(f32[96,128,128]{2,0,1:T(8,128)} %copy_bitcast_fusion.3, s32[1024]{0:T(1024)S(1)} %pad_clamp_fusion), kind=kCustom, calls=%fused_computation.1.clone | custom fusion | bytes 17302208 | tf_op jit(solution)/shard_map/jit(_take)/gather | solution.py:15
  89.3 27.0 %fusion.37 = f32[96,176,128]{2,0,1:T(8,128)S(1)} fusion(f32[1,1,176,128,128]{4,3,2,1,0:T(8,128)} %param.12, f32[176,96,128]{2,1,0:T(8,128)} %gather_fusion.1, pred[176]{0:T(512)(128)(4,1)S(1)} %get-tuple-element.8), kind=kOutput, calls=%fused_computation.41 | convolution fusion | flops 3324051456 | bytes 28836016 | tf_op jit(solution)/shard_map/sij,vsj->vsi/dot_general | solution.py:16
  116.3 11.5 %fusion.58 = f32[96,64,128]{2,1,0:T(8,128)} fusion(f32[96,176,128]{2,0,1:T(8,128)S(1)} %fusion.37, f32[176]{0:T(256)S(1)} %compare_convert_fusion.1, s32[176]{0:T(256)S(1)} %bitcast.149), kind=kOutput, calls=%fused_computation.48 | convolution fusion | flops 1660966912 | bytes 11797888 | tf_op jit(solution)/shard_map/rs,vsi->vri/dot_general | solution.py:27
  154.7 14.3 %fusion.32 = f32[96,176,128]{2,0,1:T(8,128)S(1)} fusion(f32[1,1,176,128,128]{4,3,2,1,0:T(8,128)} %param.12, f32[176,96,128]{2,1,0:T(8,128)} %gather_fusion, pred[176]{0:T(512)(128)(4,1)S(1)} %get-tuple-element.6), kind=kOutput, calls=%fused_computation.40 | convolution fusion | flops 3324051456 | bytes 28836016 | tf_op jit(solution)/shard_map/sij,vsi->vsj/dot_general | solution.py:18
  169.0 28.0 %fusion.52 = f32[96,128,128]{1,2,0:T(8,128)} fusion(f32[96,176,128]{2,0,1:T(8,128)S(1)} %fusion.32, f32[176]{0:T(256)S(1)} %compare_convert_fusion.1, s32[176]{0:T(256)S(1)} %bitcast.154), kind=kOutput, calls=%fused_computation.46 | convolution fusion | flops 3321933824 | bytes 14943616 | tf_op jit(solution)/shard_map/cs,vsj->vcj/dot_general | solution.py:28
  197.0 6.6 %copy.59 = f32[96,128,128]{2,1,0:T(8,128)} copy(f32[96,128,128]{1,2,0:T(8,128)} %fusion.52) | data formatting | bytes 12582912 | tf_op jit(solution)/shard_map/cs,vsj->vcj/transpose | solution.py:28
  203.5 9.8 %copy.104 = f32[12,8,128,128]{3,1,2,0:T(8,128)} copy(f32[12,8,128,128]{3,2,1,0:T(8,128)} %bitcast.131) | data formatting | bytes 12582912
  220.0 23.5 %all-to-all-done.2 = f32[8,96,512]{2,1,0:T(8,128)S(1)} async-done(((f32[8,96,512]{2,1,0:T(8,128)}), f32[8,96,512]{2,1,0:T(8,128)S(1)}, u32[]{:S(2)}, u32[]{:S(2)}) %all-to-all-start.2) | async-done | bytes 1572896 | tf_op jit(solution)/shard_map/all_to_all | solution.py:57
  249.3 15.6 %all-to-all-done.3 = f32[4,96,512]{2,1,0:T(8,128)S(1)} async-done(((f32[4,96,512]{2,1,0:T(8,128)}), f32[4,96,512]{2,1,0:T(8,128)S(1)}, u32[]{:S(2)}, u32[]{:S(2)}) %all-to-all-start.3) | async-done | bytes 786464 | tf_op jit(solution)/shard_map/all_to_all | solution.py:64
  265.0 8.8 %reduce-scatter.5.cloned.1.call-done = f32[96,2048]{1,0:T(8,128)} async-done(((f32[96,16384]{1,0:T(8,128)}), f32[96,2048]{1,0:T(8,128)}) %reduce-scatter.5.cloned.1.call-update) | async-done | bytes 786448 | tf_op jit(solution)/shard_map/reduce_scatter | solution.py:79
  277.3 24.5 %all_to_all.40 = f32[4,96,512]{2,1,0:T(8,128)S(1)} all-to-all(f32[4,96,512]{2,1,0:T(8,128)S(1)} %bitcast.143), channel_id=1, replica_groups=mesh['row'=8,'col'=4] {'col'}, dimensions={0} | all-to-all | bytes 1572864 | tf_op jit(solution)/shard_map/all_to_all | solution.py:36
  302.0 35.5 %all_to_all.41 = f32[8,96,512]{2,1,0:T(8,128)S(1)} all-to-all(f32[8,96,512]{2,1,0:T(8,128)S(1)} %bitcast_multiply_fusion.1), channel_id=1, replica_groups=mesh['row'=8,'col'=4] {'row'}, dimensions={0} | all-to-all | bytes 3145728 | tf_op jit(solution)/shard_map/all_to_all | solution.py:40
  345.0 7.6 %gather_fusion.3 = f32[176,96,128]{2,1,0:T(8,128)} fusion(f32[96,128,128]{2,0,1:T(8,128)} %copy_bitcast_fusion.2, s32[1024]{0:T(1024)S(1)} %pad_clamp_fusion), kind=kCustom, calls=%fused_computation.3.clone | custom fusion | bytes 17302208 | tf_op jit(solution)/shard_map/jit(_take)/gather | solution.py:15
  352.6 27.1 %fusion.47 = f32[96,176,128]{2,0,1:T(8,128)S(1)} fusion(f32[1,1,176,128,128]{4,3,2,1,0:T(8,128)} %param.12, f32[176,96,128]{2,1,0:T(8,128)} %gather_fusion.3, pred[176]{0:T(512)(128)(4,1)S(1)} %get-tuple-element.8), kind=kOutput, calls=%fused_computation.43 | convolution fusion | flops 3324051456 | bytes 28836016 | tf_op jit(solution)/shard_map/sij,vsj->vsi/dot_general | solution.py:16
  379.8 11.5 %fusion.61 = f32[96,64,128]{2,1,0:T(8,128)} fusion(f32[96,176,128]{2,0,1:T(8,128)S(1)} %fusion.47, f32[176]{0:T(256)S(1)} %compare_convert_fusion.1, s32[176]{0:T(256)S(1)} %bitcast.151), kind=kOutput, calls=%fused_computation.49 | convolution fusion | flops 1660966912 | bytes 11797888 | tf_op jit(solution)/shard_map/rs,vsi->vri/dot_general | solution.py:27
  418.8 14.3 %fusion.42 = f32[96,176,128]{2,0,1:T(8,128)S(1)} fusion(f32[1,1,176,128,128]{4,3,2,1,0:T(8,128)} %param.12, f32[176,96,128]{2,1,0:T(8,128)} %gather_fusion.2, pred[176]{0:T(512)(128)(4,1)S(1)} %get-tuple-element.6), kind=kOutput, calls=%fused_computation.42 | convolution fusion | flops 3324051456 | bytes 28836016 | tf_op jit(solution)/shard_map/sij,vsi->vsj/dot_general | solution.py:18
  433.1 28.1 %fusion.55 = f32[96,128,128]{1,2,0:T(8,128)} fusion(f32[96,176,128]{2,0,1:T(8,128)S(1)} %fusion.42, f32[176]{0:T(256)S(1)} %compare_convert_fusion.1, s32[176]{0:T(256)S(1)} %bitcast.155), kind=kOutput, calls=%fused_computation.47 | convolution fusion | flops 3321933824 | bytes 14943616 | tf_op jit(solution)/shard_map/cs,vsj->vcj/dot_general | solution.py:28
  461.2 6.6 %copy.68 = f32[96,128,128]{2,1,0:T(8,128)} copy(f32[96,128,128]{1,2,0:T(8,128)} %fusion.55) | data formatting | bytes 12582912 | tf_op jit(solution)/shard_map/cs,vsj->vcj/transpose | solution.py:28
  467.8 9.8 %copy.103 = f32[12,8,128,128]{3,1,2,0:T(8,128)} copy(f32[12,8,128,128]{3,2,1,0:T(8,128)} %bitcast.132) | data formatting | bytes 12582912
  479.1 25.7 %all_to_all.42 = f32[8,96,512]{2,1,0:T(8,128)S(1)} all-to-all(f32[8,96,512]{2,1,0:T(8,128)S(1)} %bitcast_multiply_fusion), channel_id=1, replica_groups=mesh['row'=8,'col'=4] {'row'}, dimensions={0} | all-to-all | bytes 3145728 | tf_op jit(solution)/shard_map/all_to_all | solution.py:57
  504.9 21.1 %all_to_all.43 = f32[4,96,512]{2,1,0:T(8,128)S(1)} all-to-all(f32[4,96,512]{2,1,0:T(8,128)S(1)} %dynamic-slice_bitcast_fusion), channel_id=1, replica_groups=mesh['row'=8,'col'=4] {'col'}, dimensions={0} | all-to-all | bytes 1572864 | tf_op jit(solution)/shard_map/all_to_all | solution.py:64
  526.0 12.0 %reduce-scatter.9.cloned.1.call-done = f32[96,2048]{1,0:T(8,128)} async-done(((f32[96,16384]{1,0:T(8,128)}), f32[96,2048]{1,0:T(8,128)}) %reduce-scatter.9.cloned.1.call-update) | async-done | bytes 786448 | tf_op jit(solution)/shard_map/reduce_scatter | solution.py:79
  (77 shorter events, 103.0 us)
Async XLA Ops:
  6.5 68.6 %copy-start.4 = (s32[1,1,176]{2,1,0:T(1,128)S(1)}, s32[1,1,176]{2,1,0:T(1,128)}, u32[]{:S(2)}) copy-start(s32[1,1,176]{2,1,0:T(1,128)} %param.14) | copy-start | bytes 2116
  6.5 68.6 %copy-start.3 = (s32[1,1,176]{2,1,0:T(1,128)S(1)}, s32[1,1,176]{2,1,0:T(1,128)}, u32[]{:S(2)}) copy-start(s32[1,1,176]{2,1,0:T(1,128)} %param.13) | copy-start | bytes 2116
  6.5 68.6 %all-gather.7.cloned.1.call-start = ((), (), s32[]{:S(2)}) async-start(), calls=%async_computation.13 | async-start | bytes 7077888 | tf_op jit(solution)/shard_map/all_gather | solution.py:69
  10.0 26.4 %all-to-all-start = ((f32[4,96,512]{2,1,0:T(8,128)}), f32[4,96,512]{2,1,0:T(8,128)S(1)}, u32[]{:S(2)}, u32[]{:S(2)}) async-start(f32[4,96,512]{2,1,0:T(8,128)} %copy.55), calls=%async_computation | async-start | bytes 1572864 | tf_op jit(solution)/shard_map/all_to_all | solution.py:36
  37.9 35.5 %all-to-all-start.1 = ((f32[8,96,512]{2,1,0:T(8,128)}), f32[8,96,512]{2,1,0:T(8,128)S(1)}, u32[]{:S(2)}, u32[]{:S(2)}) async-start(f32[8,96,512]{2,1,0:T(8,128)} %bitcast_multiply_fusion.3), calls=%async_computation.1 | async-start | bytes 3145728 | tf_op jit(solution)/shard_map/all_to_all | solution.py:40
  41.6 97.8 %all-gather.11.cloned.1.call-start = ((), (), s32[]{:S(2)}) async-start(), calls=%async_computation.18 | async-start | bytes 3932160 | tf_op jit(solution)/shard_map/all_gather | solution.py:42
  74.4 139.2 %reduce-scatter.7.cloned.1.call-start = ((), (), s32[]{:S(2)}) async-start(), calls=%async_computation.14 | async-start | bytes 3932160 | tf_op jit(solution)/shard_map/reduce_scatter | solution.py:52
  134.8 139.0 %reduce-scatter.5.cloned.1.call-start = ((), (), s32[]{:S(2)}) async-start(), calls=%async_computation.12 | async-start | bytes 7077888 | tf_op jit(solution)/shard_map/reduce_scatter | solution.py:79
  213.3 60.5 %copy-start = (f32[96,2048]{1,0:T(8,128)S(1)}, f32[96,2048]{1,0:T(8,128)}, u32[]{:S(2)}) copy-start(f32[96,2048]{1,0:T(8,128)} %param.11) | copy-start | bytes 2359300
  216.1 27.4 %all-to-all-start.2 = ((f32[8,96,512]{2,1,0:T(8,128)}), f32[8,96,512]{2,1,0:T(8,128)S(1)}, u32[]{:S(2)}, u32[]{:S(2)}) async-start(f32[8,96,512]{2,1,0:T(8,128)} %bitcast_multiply_fusion.2), calls=%async_computation.4 | async-start | bytes 3145728 | tf_op jit(solution)/shard_map/all_to_all | solution.py:57
  244.4 20.5 %all-to-all-start.3 = ((f32[4,96,512]{2,1,0:T(8,128)}), f32[4,96,512]{2,1,0:T(8,128)S(1)}, u32[]{:S(2)}, u32[]{:S(2)}) async-start(f32[4,96,512]{2,1,0:T(8,128)} %dynamic-slice_bitcast_fusion.1), calls=%async_computation.5 | async-start | bytes 1572864 | tf_op jit(solution)/shard_map/all_to_all | solution.py:64
  247.9 90.7 %all-gather.9.cloned.1.call-start = ((), (), s32[]{:S(2)}) async-start(), calls=%async_computation.16 | async-start | bytes 7077888 | tf_op jit(solution)/shard_map/all_gather | solution.py:69
  276.0 127.6 %all-gather.13.cloned.1.call-start = ((), (), s32[]{:S(2)}) async-start(), calls=%async_computation.19 | async-start | bytes 3932160 | tf_op jit(solution)/shard_map/all_gather | solution.py:42
  338.6 139.1 %reduce-scatter.11.cloned.1.call-start = ((), (), s32[]{:S(2)}) async-start(), calls=%async_computation.17 | async-start | bytes 3932160 | tf_op jit(solution)/shard_map/reduce_scatter | solution.py:52
  398.1 139.9 %reduce-scatter.9.cloned.1.call-start = ((), (), s32[]{:S(2)}) async-start(), calls=%async_computation.15 | async-start | bytes 7077888 | tf_op jit(solution)/shard_map/reduce_scatter | solution.py:79
  477.6 60.5 %copy-start.1 = (f32[96,2048]{1,0:T(8,128)S(1)}, f32[96,2048]{1,0:T(8,128)}, u32[]{:S(2)}) copy-start(f32[96,2048]{1,0:T(8,128)} %param.11) | copy-start | bytes 2359300
  477.6 60.5 %copy-start.2 = (f32[96,2048]{1,0:T(8,128)S(1)}, f32[96,2048]{1,0:T(8,128)}, u32[]{:S(2)}) copy-start(f32[96,2048]{1,0:T(8,128)} %subtract_divide_fusion) | copy-start | bytes 2359300
Sparse Core Ops, SparseCore 0:
  9.3 60.8 all-gather.6
  74.5 64.9 all-gather.10
  141.8 58.8 reduce-scatter.6
  213.5 60.3 reduce-scatter.4
  276.1 60.9 all-gather.8
  338.7 64.8 all-gather.12
  406.0 58.8 reduce-scatter.10
  477.7 60.2 reduce-scatter.8
where the time goes:
time: 554 us; the launch traced here: 548 us
  matrix products  162 us (29%)
  waiting for transfers between devices  123 us (22%)
  local copies, waits for them, and re-layouts  112 us (20%)
  blocking collectives  107 us (19%)
  starting transfers between devices  17.7 us (3%)
  between operations  16.1 us (3%)
  other arithmetic  10.2 us (2%)
    dot_general x2, matrix products, local_products(): jnp.einsum('cs,vsj->vcj', col_onehot, backward, precision=lax.Precision.H...  56 us
    dot_general x2, matrix products, local_products(): jnp.einsum('sij,vsj->vsi', device_blocks, source_col, precision=lax.Preci...  54.1 us
    all_to_all x1, blocking collectives, mirrored_tile(): lax.all_to_all(slots, 'row', split_axis=0, concat_axis=0, tiled=True)  35.5 us
    all_to_all x1, waiting for transfers between devices, mirrored_tile(): lax.all_to_all(slots, 'row', split_axis=0, concat_axis=0, tiled=True)  31.7 us
    dot_general x2, matrix products, local_products(): jnp.einsum('sij,vsi->vsj', device_blocks, source_row, precision=lax.Preci...  28.6 us
    all_to_all x1, blocking collectives, mirrored_sums(): lax.all_to_all(slots, 'row', split_axis=0, concat_axis=0, tiled=True)  25.7 us
    all_to_all x1, blocking collectives, mirrored_tile(): lax.all_to_all(items, 'col', split_axis=0, concat_axis=0, tiled=True)  24.5 us
    all_to_all x1, waiting for transfers between devices, mirrored_sums(): lax.all_to_all(slots, 'row', split_axis=0, concat_axis=0, tiled=True)  23.5 us
  transfers between devices with their start and end apart: 12, of which 8 were waited for; matrix products, arithmetic and copies ran while one was open for 51% of the time, Pallas kernels for 0%

commit v1 on v0

v1 whole, which is shorter than its diff:
```python
import functools

import jax
import jax.numpy as jnp
from jax import lax
from jax.experimental import pallas as pl
from jax.experimental.pallas import tpu as pltpu
from jax.sharding import PartitionSpec as P

BS = 128
VMEM_BYTES = 56 * 1024 * 1024
MESH = pl.DeviceIdType.MESH


def parts_of(total, most):
    best = 1
    for size in range(1, most + 1):
        if total % size == 0:
            best = size
    return best


def remote(src, dst, send_sem, recv_sem, row, col):
    return pltpu.make_async_remote_copy(
        src_ref=src,
        dst_ref=dst,
        send_sem=send_sem,
        recv_sem=recv_sem,
        device_id=(row, col),
        device_id_type=MESH,
    )


def gather_kernel(rows, chunks, x_ref, out_ref, local_sem, send_sem, recv_sem, fsend_sem, frecv_sem):
    half = rows // 2
    size = x_ref.shape[0]
    step = size // chunks
    r, c = lax.axis_index("row"), lax.axis_index("col")
    q, k = r // 2, r % 2
    sibling = r + 1 - 2 * k
    barrier = pltpu.get_barrier_semaphore()
    for d in range(1, half):
        pl.semaphore_signal(barrier, inc=1, device_id=((q + d) % half * 2 + k, c), device_id_type=MESH)
    pl.semaphore_signal(barrier, inc=1, device_id=(sibling, c), device_id_type=MESH)
    pl.semaphore_wait(barrier, half)

    def slot(owner, j):
        return out_ref.at[pl.ds(owner * size + j * step, step)]

    def send(d, j):
        return remote(x_ref.at[pl.ds(j * step, step)], slot(r, j), send_sem.at[d, j], recv_sem.at[d, j],
                      (q + d) % half * 2 + k, c)

    def pass_on(d, j):
        owner = (q + half - d) % half * 2 + k
        source = x_ref.at[pl.ds(j * step, step)] if d == 0 else slot(owner, j)
        return remote(source, slot(owner, j), fsend_sem.at[d, j], frecv_sem.at[d, j], sibling, c)

    for j in range(chunks):
        for d in range(1, half):
            send(d, j).start()
    for j in range(chunks):
        pass_on(0, j).start()
    own = pltpu.make_async_copy(x_ref, out_ref.at[pl.ds(r * size, size)], local_sem)
    own.start()
    for j in range(chunks):
        for d in range(1, half):
            send(d, j).wait_recv()
            pass_on(d, j).start()
    own.wait()
    for j in range(chunks):
        for d in range(half):
            pass_on(d, j).wait_recv()
            pass_on(d, j).wait_send()
            if d > 0:
                send(d, j).wait_send()


def gather(x, rows):
    size = x.shape[0]
    chunks = size // parts_of(size, max(1, size // 4))
    half = rows // 2
    return pl.pallas_call(
        functools.partial(gather_kernel, rows, chunks),
        out_shape=jax.ShapeDtypeStruct((rows * size,) + x.shape[1:], jnp.float32),
        in_specs=[pl.BlockSpec(memory_space=pltpu.VMEM)],
        out_specs=pl.BlockSpec(memory_space=pltpu.VMEM),
        scratch_shapes=[
            pltpu.SemaphoreType.DMA,
            pltpu.SemaphoreType.DMA((half, chunks)),
            pltpu.SemaphoreType.DMA((half, chunks)),
            pltpu.SemaphoreType.DMA((half, chunks)),
            pltpu.SemaphoreType.DMA((half, chunks)),
        ],
        compiler_params=pltpu.CompilerParams(
            collective_id=0, has_side_effects=True, vmem_limit_bytes=VMEM_BYTES
        ),
        name="gather",
    )(x)


def scatter_kernel(rows, chunks, g_ref, out_ref, pair, arrived, ssend_sem, srecv_sem, send_sem, recv_sem):
    half = rows // 2
    size = out_ref.shape[0]
    step = size // chunks
    r, c = lax.axis_index("row"), lax.axis_index("col")
    q, k = r // 2, r % 2
    sibling = r + 1 - 2 * k
    barrier = pltpu.get_barrier_semaphore()
    for d in range(1, half):
        pl.semaphore_signal(barrier, inc=1, device_id=((q + d) % half * 2 + k, c), device_id_type=MESH)
    pl.semaphore_signal(barrier, inc=1, device_id=(sibling, c), device_id_type=MESH)
    pl.semaphore_wait(barrier, half)

    def part(d, j, core):
        return pl.ds(((q + d) % half * 2 + core) * size + j * step, step)

    def to_sibling(d, j):
        return remote(g_ref.at[part(d, j, 1 - k)], pair.at[d, pl.ds(j * step, step)],
                      ssend_sem.at[d, j], srecv_sem.at[d, j], sibling, c)

    def send(d, j):
        return remote(pair.at[d, pl.ds(j * step, step)], arrived.at[d - 1, pl.ds(j * step, step)],
                      send_sem.at[d, j], recv_sem.at[d, j], (q + d) % half * 2 + k, c)

    order = list(range(1, half)) + [0]
    for j in range(chunks):
        for d in order:
            to_sibling(d, j).start()
    for j in range(chunks):
        here = pl.ds(j * step, step)
        for d in order:
            to_sibling(d, j).wait_recv()
            if d > 0:
                pair[d, here] = pair[d, here] + g_ref[part(d, j, k)]
                send(d, j).start()
            else:
                out_ref[here] = pair[0, here] + g_ref[part(0, j, k)]
    for j in range(chunks):
        here = pl.ds(j * step, step)
        total = out_ref[here]
        for d in range(1, half):
            send(d, j).wait_recv()
            total = total + arrived[d - 1, here]
        out_ref[here] = total
    for j in range(chunks):
        for d in range(half):
            to_sibling(d, j).wait_send()
            if d > 0:
                send(d, j).wait_send()


def scatter(g, rows):
    size = g.shape[0] // rows
    chunks = size // parts_of(size, max(1, size // 4))
    half = rows // 2
    tail = g.shape[1:]
    return pl.pallas_call(
        functools.partial(scatter_kernel, rows, chunks),
        out_shape=jax.ShapeDtypeStruct((size,) + tail, jnp.float32),
        in_specs=[pl.BlockSpec(memory_space=pltpu.VMEM)],
        out_specs=pl.BlockSpec(memory_space=pltpu.VMEM),
        scratch_shapes=[
            pltpu.VMEM((half, size) + tail, jnp.float32),
            pltpu.VMEM((half - 1, size) + tail, jnp.float32),
            pltpu.SemaphoreType.DMA((half, chunks)),
            pltpu.SemaphoreType.DMA((half, chunks)),
            pltpu.SemaphoreType.DMA((half, chunks)),
            pltpu.SemaphoreType.DMA((half, chunks)),
        ],
        compiler_params=pltpu.CompilerParams(
            collective_id=2, has_side_effects=True, vmem_limit_bytes=VMEM_BYTES
        ),
        name="scatter",
    )(g)


def chain_kernel(cols, ratio, chunks, x_ref, f_ref, row_ref, sum_ref, high, low, local_sem,
                 up_sem, down_sem, arrive_sem, rsend_sem, high_sem, low_sem):
    size = row_ref.shape[0]
    step = size // chunks
    r, c = lax.axis_index("row"), lax.axis_index("col")
    root = r // ratio
    base = r % ratio * size
    has_up, has_down = c < cols - 1, c > 0
    is_root, above, below = c == root, c > root, c < root
    barrier = pltpu.get_barrier_semaphore()

    @pl.when(has_up)
    def _():
        pl.semaphore_signal(barrier, inc=1, device_id=(r, c + 1), device_id_type=MESH)

    @pl.when(has_down)
    def _():
        pl.semaphore_signal(barrier, inc=1, device_id=(r, c - 1), device_id_type=MESH)

    pl.semaphore_wait(barrier, jnp.where(has_up, 1, 0) + jnp.where(has_down, 1, 0))

    def at(j):
        return pl.ds(j * step, step)

    def spread(source, sem, j, to):
        return remote(source, row_ref.at[at(j)], sem.at[j], arrive_sem.at[j], r, to)

    def spread_up(source, j):
        return spread(source, up_sem, j, c + 1)

    def spread_down(source, j):
        return spread(source, down_sem, j, c - 1)

    def sum_down(source, j):
        return remote(source.at[at(j)], high.at[at(j)], rsend_sem.at[j], high_sem.at[j], r, c - 1)

    def sum_up(source, j):
        return remote(source.at[at(j)], low.at[at(j)], rsend_sem.at[j], low_sem.at[j], r, c + 1)

    own = pltpu.make_async_copy(x_ref.at[pl.ds(base, size)], row_ref, local_sem)

    @pl.when(is_root)
    def _():
        for j in range(chunks):
            source = x_ref.at[pl.ds(base + j * step, step)]

            @pl.when(has_up)
            def _():
                spread_up(source, j).start()

            @pl.when(has_down)
            def _():
                spread_down(source, j).start()

        own.start()

    @pl.when(jnp.logical_and(above, c == cols - 1))
    def _():
        for j in range(chunks):
            sum_down(f_ref, j).start()

    @pl.when(jnp.logical_and(below, c == 0))
    def _():
        for j in range(chunks):
            sum_up(f_ref, j).start()

    for j in range(chunks):
        here = row_ref.at[at(j)]

        @pl.when(jnp.logical_not(is_root))
        def _():
            spread_up(here, j).wait_recv()

        @pl.when(jnp.logical_and(above, has_up))
        def _():
            spread_up(here, j).start()
            sum_down(f_ref, j).wait_recv()
            sum_ref[at(j)] = f_ref[at(j)] + high[at(j)]
            sum_down(sum_ref, j).start()

        @pl.when(jnp.logical_and(below, has_down))
        def _():
            spread_down(here, j).start()
            sum_up(f_ref, j).wait_recv()
            sum_ref[at(j)] = f_ref[at(j)] + low[at(j)]
            sum_up(sum_ref, j).start()

        @pl.when(is_root)
        def _():
            sum_ref[at(j)] = f_ref[at(j)]

            @pl.when(has_up)
            def _():
                sum_down(f_ref, j).wait_recv()
                sum_ref[at(j)] = sum_ref[at(j)] + high[at(j)]

            @pl.when(has_down)
            def _():
                sum_up(f_ref, j).wait_recv()
                sum_ref[at(j)] = sum_ref[at(j)] + low[at(j)]

    @pl.when(is_root)
    def _():
        own.wait()

    for j in range(chunks):
        here = row_ref.at[at(j)]

        @pl.when(jnp.logical_and(has_up, jnp.logical_or(is_root, above)))
        def _():
            spread_up(here, j).wait_send()

        @pl.when(jnp.logical_and(has_down, jnp.logical_or(is_root, below)))
        def _():
            spread_down(here, j).wait_send()

        @pl.when(jnp.logical_not(is_root))
        def _():
            sum_down(f_ref, j).wait_send()


def chain(x, f, cols, ratio):
    size = f.shape[0]
    chunks = size // parts_of(size, max(1, size // 8))
    whole = pl.BlockSpec(memory_space=pltpu.VMEM)
    shape = jax.ShapeDtypeStruct(f.shape, jnp.float32)
    sems = [pltpu.SemaphoreType.DMA((chunks,))] * 6
    return pl.pallas_call(
        functools.partial(chain_kernel, cols, ratio, chunks),
        out_shape=(shape, shape),
        in_specs=[whole, whole],
        out_specs=(whole, whole),
        scratch_shapes=[
            pltpu.VMEM(f.shape, jnp.float32),
            pltpu.VMEM(f.shape, jnp.float32),
            pltpu.SemaphoreType.DMA,
        ]
        + sems,
        compiler_params=pltpu.CompilerParams(
            collective_id=1, has_side_effects=True, vmem_limit_bytes=VMEM_BYTES
        ),
        name="chain",
    )(x, f)


def split(a):
    high = a.astype(jnp.bfloat16)
    return high, (a - high.astype(jnp.float32)).astype(jnp.bfloat16)


def product(x, a, contract):
    dims = (((1,), (contract,)), ((), ()))
    rows = x.shape[0]
    xh, xl = split(x)
    ah, al = split(a)
    both = lax.dot_general(jnp.concatenate([xh, xl], axis=0), ah, dims, preferred_element_type=jnp.float32)
    rest = lax.dot_general(xh, al, dims, preferred_element_type=jnp.float32)
    return both[:rows] + (both[rows:] + rest)


def products_kernel(group, contract, take_ref, put_ref, info_ref, x_ref, blocks_ref, *rest):
    out_ref = rest[-1]
    slots = blocks_ref.shape[0]
    first = pl.program_id(0) * slots
    count = info_ref[0]

    @pl.when(pl.program_id(0) == 0)
    def _():
        out_ref[...] = jnp.zeros_like(out_ref)
        if len(rest) == 2:
            add_ref = rest[0]

            @pl.when(info_ref[1] == 1)
            def _():
                out_ref[pl.ds(info_ref[2], add_ref.shape[0])] = add_ref[...]

    live = jnp.clip(count - first, 0, slots)

    def step(i, carry):
        at = i * group
        results = []
        for u in range(group):
            result = product(x_ref[take_ref[first + at + u]], blocks_ref[at + u], contract)
            results.append(jnp.where(at + u < live, result, 0.0))
        for u in range(group):
            place = put_ref[first + at + u]
            out_ref[place] = out_ref[place] + results[u]
        return carry

    lax.fori_loop(0, (live + group - 1) // group, step, 0)


def products(take, put, info, x, blocks, contract, out_blocks, add=None):
    total = blocks.shape[0]
    slots = parts_of(total, 44)
    group = parts_of(slots, 4)
    vecs = x.shape[1]
    whole = pl.BlockSpec(memory_space=pltpu.VMEM)
    in_specs = [whole, pl.BlockSpec((slots, BS, BS), lambda i, *_: (i, 0, 0))]
    operands = [x, blocks]
    if add is not None:
        in_specs.append(whole)
        operands.append(add)
    return pl.pallas_call(
        functools.partial(products_kernel, group, contract),
        out_shape=jax.ShapeDtypeStruct((out_blocks, vecs, BS), jnp.float32),
        grid_spec=pltpu.PrefetchScalarGridSpec(
            num_scalar_prefetch=3,
            grid=(total // slots,),
            in_specs=in_specs,
            out_specs=whole,
        ),
        compiler_params=pltpu.CompilerParams(vmem_limit_bytes=VMEM_BYTES),
        name="products",
    )(take, put, info, *operands)


def body(rows, cols, vectors, blocks, block_row, block_col, block_count, lower_bound, upper_bound):
    device_blocks = blocks[0, 0]
    rows_local, cols_local = block_row[0, 0], block_col[0, 0]
    ratio = rows // cols
    vecs, piece = vectors.shape
    col_blocks = piece * rows // BS
    row_blocks = piece * cols // BS
    row_index, col_index = lax.axis_index("row"), lax.axis_index("col")
    info = jnp.stack(
        [
            block_count[0, 0],
            (row_index // ratio == col_index).astype(jnp.int32),
            (row_index % ratio * row_blocks).astype(jnp.int32),
        ]
    )
    center = (upper_bound[0] + lower_bound[0]) / 2.0
    half_width = (upper_bound[0] - lower_bound[0]) / 2.0

    def apply_hamiltonian(x):
        col_tile = gather(x, rows)
        forward = products(cols_local, rows_local, info, col_tile, device_blocks, 1, row_blocks)
        row_tile, summed = chain(col_tile, forward, cols, ratio)
        backward = products(
            rows_local, cols_local, info, row_tile, device_blocks, 0, col_blocks, summed
        )
        return scatter(backward, rows)

    start = jnp.transpose(vectors.reshape(vecs, piece // BS, BS), (1, 0, 2))
    current = (apply_hamiltonian(start) - center * start) / half_width
    following = 2.0 * (apply_hamiltonian(current) - center * current) / half_width - start
    return jnp.transpose(following, (1, 0, 2)).reshape(vecs, piece)


def solution(mesh):
    placed = (
        P(None, ("col", "row")),
        P("row", "col", None, None, None),
        P("row", "col", None),
        P("row", "col", None),
        P("row", "col"),
        P(),
        P(),
    )
    return jax.shard_map(
        functools.partial(body, mesh.shape["row"], mesh.shape["col"]),
        mesh=mesh,
        in_specs=placed,
        out_specs=P(None, ("col", "row")),
        check_vma=False,
    )
```

time: 554 us -> 562 us (1.014); the launches traced: 548 us -> 568 us
  Pallas kernels: 0 us -> 559 us
  matrix products: 162 us -> 0 us
  waiting for transfers between devices: 123 us -> 0 us
  local copies, waits for them, and re-layouts: 112 us -> 0.97 us
  blocking collectives: 107 us -> 0 us
  starting transfers between devices: 17.7 us -> 0 us
  between operations: 16.1 us -> 2.08 us
    pallas_call x0 -> x10, Pallas kernels: none -> 559 us  [the longest x2 314 us: chain(): pl.pallas_call(functools.partial(chain_kernel, cols, ratio, chunks), out_...]
    dot_general x8 -> x0, matrix products: 162 us -> none  [the longest x2 56 us: local_products(): jnp.einsum('cs,vsj->vcj', col_onehot, backward, precision=lax.Precision.H...]
    all_to_all x4 -> x0, blocking collectives: 107 us -> none  [the longest x1 35.5 us: mirrored_tile(): lax.all_to_all(slots, 'row', split_axis=0, concat_axis=0, tiled=True)]
    all_to_all x4 -> x0, waiting for transfers between devices: 90.9 us -> none  [the longest x1 31.7 us: mirrored_tile(): lax.all_to_all(slots, 'row', split_axis=0, concat_axis=0, tiled=True)]
    another operation x8 -> x0, local copies, waits for them, and re-layouts: 27.4 us -> none  [the longest x4 13.8 us: mirrored_sums(): forward_part.reshape(vector_count, col_count, col_count, sub_width)]
    gather x4 -> x0, local copies, waits for them, and re-layouts: 24.3 us -> none  [the longest x2 15.4 us: local_products(): source_col = jnp.take(col_view, cols_local, axis=1)]
    transpose x5 -> x1, local copies, waits for them, and re-layouts: 22.1 us -> 0.96 us  [body(): start = jnp.transpose(vectors.reshape(vecs, piece // BS, BS), (1, 0, 2))]
    reduce_scatter x4 -> x0, waiting for transfers between devices: 20.9 us -> none  [the longest x2 20.8 us: apply_hamiltonian(): lax.psum_scatter(backward_part, 'row', scatter_dimension=1, tiled=True)]
  transfers between devices with their start and end apart: 12 -> 0, of which waited for: 8 -> 0; matrix products, arithmetic and copies ran while one was open for 51% -> 0% of each run, Pallas kernels for 0% -> 0%
where the time goes in v1:
time: 562 us; the launch traced here: 568 us
  Pallas kernels  559 us (99%)
    pallas_call x2, Pallas kernels, chain(): pl.pallas_call(functools.partial(chain_kernel, cols, ratio, chunks), out_...  314 us
    pallas_call x2, Pallas kernels, gather(): pl.pallas_call(functools.partial(gather_kernel, rows, chunks), out_shape=...  87.7 us
    pallas_call x2, Pallas kernels, scatter(): pl.pallas_call(functools.partial(scatter_kernel, rows, chunks), out_shape...  82.2 us
    pallas_call x4, Pallas kernels, products(): pl.pallas_call(functools.partial(products_kernel, group, contract), out_s...  75.2 us

profile of v1, /device:TPU:0, one launch (start us, length us, event | category | flops | bytes accessed | tf_op | source)
XLA Modules:
  0.0 567.5 jit_solution(10562778959445432917)
XLA Ops:
  0.0 0.0 copy-start
  2.0 0.7 pad_add_fusion.info_ref
  2.7 0.0 copy-done
  2.7 1.0 bitcast_bitcast_fusion.x_ref
  3.6 44.3 %gather.2.x_ref = f32[128,96,128]{2,1,0:T(8,128)} custom-call(f32[16,96,128]{2,1,0:T(8,128)} %bitcast_bitcast_fusion.x_ref), custom_call_target="tpu_custom_call" | custom-call | tf_op jit(solution)/shard_map/gather/pallas_call | solution.py:83
  47.9 19.2 %products.4.f_ref = f32[64,96,128]{2,1,0:T(8,128)} custom-call(s32[176]{0:T(256)} %bitcast.49, s32[176]{0:T(256)} %bitcast.45, s32[3]{0:T(128)} %pad_add_fusion.info_ref, f32[128,96,128]{2,1,0:T(8,128)} %gather.2.x_ref, f32[176,128,128]{2,1,0:T(8,128)} %bitcast.41), custom_call_target="tpu_custom_call" | custom-call | tf_op jit(solution)/shard_map/products/pallas_call | solution.py:381
  67.1 153.2 %chain.2 = (f32[64,96,128]{2,1,0:T(8,128)}, f32[64,96,128]{2,1,0:T(8,128)}) custom-call(f32[128,96,128]{2,1,0:T(8,128)} %gather.2.x_ref, f32[64,96,128]{2,1,0:T(8,128)} %products.4.f_ref), custom_call_target="tpu_custom_call" | custom-call | tf_op jit(solution)/shard_map/chain/pallas_call | solution.py:305
  220.3 18.4 %products.5.g_ref = f32[128,96,128]{2,1,0:T(8,128)} custom-call(s32[176]{0:T(256)} %bitcast.46, s32[176]{0:T(256)} %bitcast.50, s32[3]{0:T(128)} %pad_add_fusion.info_ref, f32[64,96,128]{2,1,0:T(8,128)} %get-tuple-element.9.x_ref, f32[176,128,128]{2,1,0:T(8,128)} %bitcast.42, f32[64,96,128]{2,1,0:T(8,128)} %get-tuple-element.10.rest_0_), custom_call_target="tpu_custom_call" | custom-call | tf_op jit(solution)/shard_map/products/pallas_call | solution.py:381
  238.7 41.1 %scatter.2 = f32[16,96,128]{2,1,0:T(8,128)} custom-call(f32[128,96,128]{2,1,0:T(8,128)} %products.5.g_ref), custom_call_target="tpu_custom_call" | custom-call | tf_op jit(solution)/shard_map/scatter/pallas_call | solution.py:158
  279.8 2.1 subtract_divide_fusion.x_ref
  282.0 43.4 %gather.3.x_ref = f32[128,96,128]{2,1,0:T(8,128)} custom-call(f32[16,96,128]{2,1,0:T(8,128)} %subtract_divide_fusion.x_ref), custom_call_target="tpu_custom_call" | custom-call | tf_op jit(solution)/shard_map/gather/pallas_call | solution.py:83
  325.3 19.2 %products.6.f_ref = f32[64,96,128]{2,1,0:T(8,128)} custom-call(s32[176]{0:T(256)} %bitcast.51, s32[176]{0:T(256)} %bitcast.47, s32[3]{0:T(128)} %pad_add_fusion.info_ref, f32[128,96,128]{2,1,0:T(8,128)} %gather.3.x_ref, f32[176,128,128]{2,1,0:T(8,128)} %bitcast.43), custom_call_target="tpu_custom_call" | custom-call | tf_op jit(solution)/shard_map/products/pallas_call | solution.py:381
  344.5 161.2 %chain.3 = (f32[64,96,128]{2,1,0:T(8,128)}, f32[64,96,128]{2,1,0:T(8,128)}) custom-call(f32[128,96,128]{2,1,0:T(8,128)} %gather.3.x_ref, f32[64,96,128]{2,1,0:T(8,128)} %products.6.f_ref), custom_call_target="tpu_custom_call" | custom-call | tf_op jit(solution)/shard_map/chain/pallas_call | solution.py:305
  505.7 18.4 %products.7.g_ref = f32[128,96,128]{2,1,0:T(8,128)} custom-call(s32[176]{0:T(256)} %bitcast.48, s32[176]{0:T(256)} %bitcast.52, s32[3]{0:T(128)} %pad_add_fusion.info_ref, f32[64,96,128]{2,1,0:T(8,128)} %get-tuple-element.11.x_ref, f32[176,128,128]{2,1,0:T(8,128)} %bitcast.44, f32[64,96,128]{2,1,0:T(8,128)} %get-tuple-element.12.rest_0_), custom_call_target="tpu_custom_call" | custom-call | tf_op jit(solution)/shard_map/products/pallas_call | solution.py:381
  524.2 0.0 copy-start.1
  524.2 41.1 %scatter.3 = f32[16,96,128]{2,1,0:T(8,128)} custom-call(f32[128,96,128]{2,1,0:T(8,128)} %products.7.g_ref), custom_call_target="tpu_custom_call" | custom-call | tf_op jit(solution)/shard_map/scatter/pallas_call | solution.py:158
  565.3 0.0 copy-done.1
  565.3 2.2 copy_bitcast_fusion
Async XLA Ops:
  0.0 2.7 copy-start
  524.2 41.1 %copy-start.1 = (f32[16,96,128]{2,1,0:T(8,128)S(1)}, f32[16,96,128]{2,1,0:T(8,128)}, u32[]{:S(2)}) copy-start(f32[16,96,128]{2,1,0:T(8,128)} %scatter.2) | copy-start | bytes 2359300

commit v2 on v1

--- a/solution.py
+++ b/solution.py
@@ -241,40 +241,61 @@
         for j in range(chunks):
             sum_up(f_ref, j).start()
 
-    for j in range(chunks):
-        here = row_ref.at[at(j)]
-
-        @pl.when(jnp.logical_not(is_root))
-        def _():
-            spread_up(here, j).wait_recv()
-
-        @pl.when(jnp.logical_and(above, has_up))
-        def _():
-            spread_up(here, j).start()
+    lag = jnp.where(above, cols - 2 - c, c - 1) * 2
+
+    def pass_on(t, carry):
+        j = t - lag
+        live = jnp.logical_and(j >= 0, j < chunks)
+
+        @pl.when(t < chunks)
+        def _():
+            here = row_ref.at[at(t)]
+            spread_up(here, t).wait_recv()
+
+            @pl.when(jnp.logical_and(above, has_up))
+            def _():
+                spread_up(here, t).start()
+
+            @pl.when(jnp.logical_and(below, has_down))
+            def _():
+                spread_down(here, t).start()
+
+        @pl.when(jnp.logical_and(live, jnp.logical_and(above, has_up)))
+        def _():
             sum_down(f_ref, j).wait_recv()
             sum_ref[at(j)] = f_ref[at(j)] + high[at(j)]
             sum_down(sum_ref, j).start()
 
-        @pl.when(jnp.logical_and(below, has_down))
-        def _():
-            spread_down(here, j).start()
+        @pl.when(jnp.logical_and(live, jnp.logical_and(below, has_down)))
+        def _():
             sum_up(f_ref, j).wait_recv()
             sum_ref[at(j)] = f_ref[at(j)] + low[at(j)]
             sum_up(sum_ref, j).start()
 
-        @pl.when(is_root)
-        def _():
-            sum_ref[at(j)] = f_ref[at(j)]
-
-            @pl.when(has_up)
-            def _():
-                sum_down(f_ref, j).wait_recv()
-                sum_ref[at(j)] = sum_ref[at(j)] + high[at(j)]
-
-            @pl.when(has_down)
-            def _():
-                sum_up(f_ref, j).wait_recv()
-                sum_ref[at(j)] = sum_ref[at(j)] + low[at(j)]
+        return carry
+
+    @pl.when(jnp.logical_not(is_root))
+    def _():
+        lax.fori_loop(0, chunks + 2 * max(cols - 3, 0), pass_on, 0)
+
+    def take_in(j, carry):
+        sum_ref[at(j)] = f_ref[at(j)]
+
+        @pl.when(has_up)
+        def _():
+            sum_down(f_ref, j).wait_recv()
+            sum_ref[at(j)] = sum_ref[at(j)] + high[at(j)]
+
+        @pl.when(has_down)
+        def _():
+            sum_up(f_ref, j).wait_recv()
+            sum_ref[at(j)] = sum_ref[at(j)] + low[at(j)]
+
+        return carry
+
+    @pl.when(is_root)
+    def _():
+        lax.fori_loop(0, chunks, take_in, 0)
 
     @pl.when(is_root)
     def _():
@@ -298,7 +319,7 @@
 
 def chain(x, f, cols, ratio):
     size = f.shape[0]
-    chunks = size // parts_of(size, max(1, size // 8))
+    chunks = size // parts_of(size, max(1, size // 16))
     whole = pl.BlockSpec(memory_space=pltpu.VMEM)
     shape = jax.ShapeDtypeStruct(f.shape, jnp.float32)
     sems = [pltpu.SemaphoreType.DMA((chunks,))] * 6

time: 562 us -> 436 us (0.78); the launches traced: 568 us -> 436 us
  Pallas kernels: 559 us -> 428 us
    pallas_call x2, Pallas kernels: 314 us -> 183 us  [chain(): pl.pallas_call(functools.partial(chain_kernel, cols, ratio, chunks), out_...]
where the time goes in v2:
time: 436 us
  Pallas kernels  428 us (98%)
  other arithmetic  5 us (1%)
    pallas_call x2, Pallas kernels, chain(): pl.pallas_call(functools.partial(chain_kernel, cols, ratio, chunks), out_...  183 us
    pallas_call x2, Pallas kernels, gather(): pl.pallas_call(functools.partial(gather_kernel, rows, chunks), out_shape=...  87.7 us
    pallas_call x2, Pallas kernels, scatter(): pl.pallas_call(functools.partial(scatter_kernel, rows, chunks), out_shape...  82.2 us
    pallas_call x4, Pallas kernels, products(): pl.pallas_call(functools.partial(products_kernel, group, contract), out_s...  75.2 us

profile of v2, /device:TPU:0, one launch (start us, length us, event | category | flops | bytes accessed | tf_op | source)
XLA Modules:
  0.0 435.8 jit_solution(15012557955793924813)
XLA Ops:
  0.0 0.0 copy-start
  2.0 0.7 pad_add_fusion.info_ref
  2.7 0.0 copy-done
  2.7 1.0 bitcast_bitcast_fusion.x_ref
  3.6 44.3 %gather.2.x_ref = f32[128,96,128]{2,1,0:T(8,128)} custom-call(f32[16,96,128]{2,1,0:T(8,128)} %bitcast_bitcast_fusion.x_ref), custom_call_target="tpu_custom_call" | custom-call | tf_op jit(solution)/shard_map/gather/pallas_call | solution.py:83
  47.9 19.2 %products.4.f_ref = f32[64,96,128]{2,1,0:T(8,128)} custom-call(s32[176]{0:T(256)} %bitcast.49, s32[176]{0:T(256)} %bitcast.45, s32[3]{0:T(128)} %pad_add_fusion.info_ref, f32[128,96,128]{2,1,0:T(8,128)} %gather.2.x_ref, f32[176,128,128]{2,1,0:T(8,128)} %bitcast.41), custom_call_target="tpu_custom_call" | custom-call | tf_op jit(solution)/shard_map/products/pallas_call | solution.py:402
  67.1 93.4 %chain.2 = (f32[64,96,128]{2,1,0:T(8,128)}, f32[64,96,128]{2,1,0:T(8,128)}) custom-call(f32[128,96,128]{2,1,0:T(8,128)} %gather.2.x_ref, f32[64,96,128]{2,1,0:T(8,128)} %products.4.f_ref), custom_call_target="tpu_custom_call" | custom-call | tf_op jit(solution)/shard_map/chain/pallas_call | solution.py:326
  160.5 18.4 %products.5.g_ref = f32[128,96,128]{2,1,0:T(8,128)} custom-call(s32[176]{0:T(256)} %bitcast.46, s32[176]{0:T(256)} %bitcast.50, s32[3]{0:T(128)} %pad_add_fusion.info_ref, f32[64,96,128]{2,1,0:T(8,128)} %get-tuple-element.9.x_ref, f32[176,128,128]{2,1,0:T(8,128)} %bitcast.42, f32[64,96,128]{2,1,0:T(8,128)} %get-tuple-element.10.rest_0_), custom_call_target="tpu_custom_call" | custom-call | tf_op jit(solution)/shard_map/products/pallas_call | solution.py:402
  178.9 41.1 %scatter.2 = f32[16,96,128]{2,1,0:T(8,128)} custom-call(f32[128,96,128]{2,1,0:T(8,128)} %products.5.g_ref), custom_call_target="tpu_custom_call" | custom-call | tf_op jit(solution)/shard_map/scatter/pallas_call | solution.py:158
  220.0 2.1 subtract_divide_fusion.x_ref
  222.1 43.4 %gather.3.x_ref = f32[128,96,128]{2,1,0:T(8,128)} custom-call(f32[16,96,128]{2,1,0:T(8,128)} %subtract_divide_fusion.x_ref), custom_call_target="tpu_custom_call" | custom-call | tf_op jit(solution)/shard_map/gather/pallas_call | solution.py:83
  265.5 19.2 %products.6.f_ref = f32[64,96,128]{2,1,0:T(8,128)} custom-call(s32[176]{0:T(256)} %bitcast.51, s32[176]{0:T(256)} %bitcast.47, s32[3]{0:T(128)} %pad_add_fusion.info_ref, f32[128,96,128]{2,1,0:T(8,128)} %gather.3.x_ref, f32[176,128,128]{2,1,0:T(8,128)} %bitcast.43), custom_call_target="tpu_custom_call" | custom-call | tf_op jit(solution)/shard_map/products/pallas_call | solution.py:402
  284.7 89.3 %chain.3 = (f32[64,96,128]{2,1,0:T(8,128)}, f32[64,96,128]{2,1,0:T(8,128)}) custom-call(f32[128,96,128]{2,1,0:T(8,128)} %gather.3.x_ref, f32[64,96,128]{2,1,0:T(8,128)} %products.6.f_ref), custom_call_target="tpu_custom_call" | custom-call | tf_op jit(solution)/shard_map/chain/pallas_call | solution.py:326
  374.0 18.4 %products.7.g_ref = f32[128,96,128]{2,1,0:T(8,128)} custom-call(s32[176]{0:T(256)} %bitcast.48, s32[176]{0:T(256)} %bitcast.52, s32[3]{0:T(128)} %pad_add_fusion.info_ref, f32[64,96,128]{2,1,0:T(8,128)} %get-tuple-element.11.x_ref, f32[176,128,128]{2,1,0:T(8,128)} %bitcast.44, f32[64,96,128]{2,1,0:T(8,128)} %get-tuple-element.12.rest_0_), custom_call_target="tpu_custom_call" | custom-call | tf_op jit(solution)/shard_map/products/pallas_call | solution.py:402
  392.4 0.0 copy-start.1
  392.4 41.1 %scatter.3 = f32[16,96,128]{2,1,0:T(8,128)} custom-call(f32[128,96,128]{2,1,0:T(8,128)} %products.7.g_ref), custom_call_target="tpu_custom_call" | custom-call | tf_op jit(solution)/shard_map/scatter/pallas_call | solution.py:158
  433.6 0.0 copy-done.1
  433.6 2.2 copy_bitcast_fusion
Async XLA Ops:
  0.0 2.7 copy-start
  392.4 41.1 %copy-start.1 = (f32[16,96,128]{2,1,0:T(8,128)S(1)}, f32[16,96,128]{2,1,0:T(8,128)}, u32[]{:S(2)}) copy-start(f32[16,96,128]{2,1,0:T(8,128)} %scatter.2) | copy-start | bytes 2359300

commit v3 on v2

--- a/solution.py
+++ b/solution.py
@@ -78,10 +78,13 @@
 
 def gather(x, rows):
     size = x.shape[0]
-    chunks = size // parts_of(size, max(1, size // 4))
     half = rows // 2
+    chunks = size // parts_of(size, max(1, size // 8))
+    kernel = functools.partial(gather_kernel, rows, chunks)
+    if half == 4:
+        kernel = functools.partial(square_gather_kernel, chunks)
     return pl.pallas_call(
-        functools.partial(gather_kernel, rows, chunks),
+        kernel,
         out_shape=jax.ShapeDtypeStruct((rows * size,) + x.shape[1:], jnp.float32),
         in_specs=[pl.BlockSpec(memory_space=pltpu.VMEM)],
         out_specs=pl.BlockSpec(memory_space=pltpu.VMEM),
@@ -152,11 +155,14 @@
 
 def scatter(g, rows):
     size = g.shape[0] // rows
-    chunks = size // parts_of(size, max(1, size // 4))
     half = rows // 2
+    chunks = size // parts_of(size, max(1, size // 8))
     tail = g.shape[1:]
+    kernel = functools.partial(scatter_kernel, rows, chunks)
+    if half == 4:
+        kernel = functools.partial(square_scatter_kernel, chunks)
     return pl.pallas_call(
-        functools.partial(scatter_kernel, rows, chunks),
+        kernel,
         out_shape=jax.ShapeDtypeStruct((size,) + tail, jnp.float32),
         in_specs=[pl.BlockSpec(memory_space=pltpu.VMEM)],
         out_specs=pl.BlockSpec(memory_space=pltpu.VMEM),
@@ -173,6 +179,126 @@
         ),
         name="scatter",
     )(g)
+
+
+def partners_of(q):
+    return [q, q + 1 - q % 2 * 2, q + 2 - q // 2 * 4, 3 - q]
+
+
+def greet_square(q, k, c, sibling):
+    barrier = pltpu.get_barrier_semaphore()
+    for d in (1, 2):
+        pl.semaphore_signal(barrier, inc=1, device_id=(partners_of(q)[d] * 2 + k, c), device_id_type=MESH)
+    pl.semaphore_signal(barrier, inc=1, device_id=(sibling, c), device_id_type=MESH)
+    pl.semaphore_wait(barrier, 3)
+
+
+def square_gather_kernel(chunks, x_ref, out_ref, local_sem, send_sem, recv_sem, fsend_sem, frecv_sem):
+    size = x_ref.shape[0]
+    step = size // chunks
+    r, c = lax.axis_index("row"), lax.axis_index("col")
+    q, k = r // 2, r % 2
+    sibling = r + 1 - 2 * k
+    partners = partners_of(q)
+    greet_square(q, k, c, sibling)
+
+    def slot(d, j):
+        return out_ref.at[pl.ds((partners[d] * 2 + k) * size + j * step, step)]
+
+    def mine(j):
+        return x_ref.at[pl.ds(j * step, step)]
+
+    def send(d, j):
+        return remote(mine(j), slot(0, j), send_sem.at[d, j], recv_sem.at[d, j], partners[d] * 2 + k, c)
+
+    def relay(j):
+        first = 1 + j % 2
+        source = slot(first, j)
+        return remote(source, source, send_sem.at[3, j], recv_sem.at[3, j], partners[3 - first] * 2 + k, c)
+
+    def pass_on(d, j):
+        source = mine(j) if d == 0 else slot(d, j)
+        return remote(source, slot(d, j), fsend_sem.at[d, j], frecv_sem.at[d, j], sibling, c)
+
+    for j in range(chunks):
+        for d in (1, 2):
+            send(d, j).start()
+    for j in range(chunks):
+        pass_on(0, j).start()
+    own = pltpu.make_async_copy(x_ref, out_ref.at[pl.ds(r * size, size)], local_sem)
+    own.start()
+    for t in range(chunks + 2):
+        if t < chunks:
+            for d in (1, 2):
+                send(d, t).wait_recv()
+                if d == 1 + t % 2:
+                    relay(t).start()
+                pass_on(d, t).start()
+        if t >= 2:
+            relay(t - 2).wait_recv()
+            pass_on(3, t - 2).start()
+    own.wait()
+    for j in range(chunks):
+        for d in range(4):
+            pass_on(d, j).wait_recv()
+            pass_on(d, j).wait_send()
+        for d in (1, 2):
+            send(d, j).wait_send()
+        relay(j).wait_send()
+
+
+def square_scatter_kernel(chunks, g_ref, out_ref, pair, arrived, ssend_sem, srecv_sem, send_sem, recv_sem):
+    size = out_ref.shape[0]
+    step = size // chunks
+    r, c = lax.axis_index("row"), lax.axis_index("col")
+    q, k = r // 2, r % 2
+    sibling = r + 1 - 2 * k
+    partners = partners_of(q)
+    greet_square(q, k, c, sibling)
+
+    def at(j):
+        return pl.ds(j * step, step)
+
+    def part(d, j, core):
+        return pl.ds((partners[d] * 2 + core) * size + j * step, step)
+
+    def to_sibling(d, j):
+        return remote(g_ref.at[part(d, j, 1 - k)], pair.at[d, at(j)],
+                      ssend_sem.at[d, j], srecv_sem.at[d, j], sibling, c)
+
+    def send(d, j):
+        to = 1 + j % 2 if d == 3 else d
+        return remote(pair.at[d, at(j)], arrived.at[d - 1, at(j)],
+                      send_sem.at[d, j], recv_sem.at[d, j], partners[to] * 2 + k, c)
+
+    for j in range(chunks):
+        for d in (3, 1 + j % 2, 2 - j % 2, 0):
+            to_sibling(d, j).start()
+    for t in range(chunks + 2):
+        if t < chunks:
+            for d in (3, 1 + t % 2, 2 - t % 2, 0):
+                to_sibling(d, t).wait_recv()
+                if d == 0:
+                    out_ref[at(t)] = pair[0, at(t)] + g_ref[part(0, t, k)]
+                else:
+                    pair[d, at(t)] = pair[d, at(t)] + g_ref[part(d, t, k)]
+                if d == 3 or d == 1 + t % 2:
+                    send(d, t).start()
+        if t >= 2:
+            j = t - 2
+            d = 2 - j % 2
+            send(3, j).wait_recv()
+            pair[d, at(j)] = pair[d, at(j)] + arrived[2, at(j)]
+            send(d, j).start()
+    for j in range(chunks):
+        send(1, j).wait_recv()
+        send(2, j).wait_recv()
+        out_ref[at(j)] = out_ref[at(j)] + (arrived[0, at(j)] + arrived[1, at(j)])
+    for j in range(chunks):
+        for d in range(4):
+            to_sibling(d, j).wait_send()
+            if d > 0:
+                send(d, j).wait_send()
 
 
 def chain_kernel(cols, ratio, chunks, x_ref, f_ref, row_ref, sum_ref, high, low, local_sem,
@@ -319,7 +445,7 @@
 
 def chain(x, f, cols, ratio):
     size = f.shape[0]
-    chunks = size // parts_of(size, max(1, size // 16))
+    chunks = size // parts_of(size, max(1, size // 32))
     whole = pl.BlockSpec(memory_space=pltpu.VMEM)
     shape = jax.ShapeDtypeStruct(f.shape, jnp.float32)
     sems = [pltpu.SemaphoreType.DMA((chunks,))] * 6

time: 436 us -> 435 us (level)
    pallas_call x2, Pallas kernels: 183 us -> 235 us  [chain(): pl.pallas_call(functools.partial(chain_kernel, cols, ratio, chunks), out_...]
    pallas_call x4, Pallas kernels: 170 us -> 144 us  [the longest x2 75.6 us: gather(): pl.pallas_call(kernel, out_shape=jax.ShapeDtypeStruct((rows * size,) + x....]
    pallas_call x4, Pallas kernels: 75.2 us -> 52 us  [products(): pl.pallas_call(functools.partial(products_kernel, group, contract), out_s...]
where the time goes in v3:
time: 435 us; the launch traced here: 439 us
  Pallas kernels  431 us (99%)
  other arithmetic  5 us (1%)
    pallas_call x2, Pallas kernels, chain(): pl.pallas_call(functools.partial(chain_kernel, cols, ratio, chunks), out_...  235 us
    pallas_call x2, Pallas kernels, gather(): pl.pallas_call(kernel, out_shape=jax.ShapeDtypeStruct((rows * size,) + x....  75.6 us
    pallas_call x2, Pallas kernels, scatter(): pl.pallas_call(kernel, out_shape=jax.ShapeDtypeStruct((size,) + tail, jnp...  68 us
    pallas_call x4, Pallas kernels, products(): pl.pallas_call(functools.partial(products_kernel, group, contract), out_s...  52 us

profile of v3, /device:TPU:0, one launch (start us, length us, event | category | flops | bytes accessed | tf_op | source)
XLA Modules:
  0.0 439.1 jit_solution(12832361625333350733)
XLA Ops:
  0.0 0.0 copy-start
  2.0 0.7 pad_add_fusion.info_ref
  2.7 0.0 copy-done
  2.7 1.0 bitcast_bitcast_fusion.x_ref
  3.6 38.8 %gather.2.x_ref = f32[128,96,128]{2,1,0:T(8,128)} custom-call(f32[16,96,128]{2,1,0:T(8,128)} %bitcast_bitcast_fusion.x_ref), custom_call_target="tpu_custom_call" | custom-call | tf_op jit(solution)/shard_map/gather/pallas_call | solution.py:86
  42.4 12.6 %products.4.f_ref = f32[64,96,128]{2,1,0:T(8,128)} custom-call(s32[176]{0:T(256)} %bitcast.49, s32[176]{0:T(256)} %bitcast.45, s32[3]{0:T(128)} %pad_add_fusion.info_ref, f32[128,96,128]{2,1,0:T(8,128)} %gather.2.x_ref, f32[176,128,128]{2,1,0:T(8,128)} %bitcast.41), custom_call_target="tpu_custom_call" | custom-call | tf_op jit(solution)/shard_map/products/pallas_call | solution.py:528
  55.1 116.2 %chain.2 = (f32[64,96,128]{2,1,0:T(8,128)}, f32[64,96,128]{2,1,0:T(8,128)}) custom-call(f32[128,96,128]{2,1,0:T(8,128)} %gather.2.x_ref, f32[64,96,128]{2,1,0:T(8,128)} %products.4.f_ref), custom_call_target="tpu_custom_call" | custom-call | tf_op jit(solution)/shard_map/chain/pallas_call | solution.py:452
  171.3 13.4 %products.5.g_ref = f32[128,96,128]{2,1,0:T(8,128)} custom-call(s32[176]{0:T(256)} %bitcast.46, s32[176]{0:T(256)} %bitcast.50, s32[3]{0:T(128)} %pad_add_fusion.info_ref, f32[64,96,128]{2,1,0:T(8,128)} %get-tuple-element.9.x_ref, f32[176,128,128]{2,1,0:T(8,128)} %bitcast.42, f32[64,96,128]{2,1,0:T(8,128)} %get-tuple-element.10.rest_0_), custom_call_target="tpu_custom_call" | custom-call | tf_op jit(solution)/shard_map/products/pallas_call | solution.py:528
  184.6 34.0 %scatter.2 = f32[16,96,128]{2,1,0:T(8,128)} custom-call(f32[128,96,128]{2,1,0:T(8,128)} %products.5.g_ref), custom_call_target="tpu_custom_call" | custom-call | tf_op jit(solution)/shard_map/scatter/pallas_call | solution.py:164
  218.6 2.1 subtract_divide_fusion.x_ref
  220.8 36.8 %gather.3.x_ref = f32[128,96,128]{2,1,0:T(8,128)} custom-call(f32[16,96,128]{2,1,0:T(8,128)} %subtract_divide_fusion.x_ref), custom_call_target="tpu_custom_call" | custom-call | tf_op jit(solution)/shard_map/gather/pallas_call | solution.py:86
  257.6 12.6 %products.6.f_ref = f32[64,96,128]{2,1,0:T(8,128)} custom-call(s32[176]{0:T(256)} %bitcast.51, s32[176]{0:T(256)} %bitcast.47, s32[3]{0:T(128)} %pad_add_fusion.info_ref, f32[128,96,128]{2,1,0:T(8,128)} %gather.3.x_ref, f32[176,128,128]{2,1,0:T(8,128)} %bitcast.43), custom_call_target="tpu_custom_call" | custom-call | tf_op jit(solution)/shard_map/products/pallas_call | solution.py:528
  270.2 119.2 %chain.3 = (f32[64,96,128]{2,1,0:T(8,128)}, f32[64,96,128]{2,1,0:T(8,128)}) custom-call(f32[128,96,128]{2,1,0:T(8,128)} %gather.3.x_ref, f32[64,96,128]{2,1,0:T(8,128)} %products.6.f_ref), custom_call_target="tpu_custom_call" | custom-call | tf_op jit(solution)/shard_map/chain/pallas_call | solution.py:452
  389.4 13.4 %products.7.g_ref = f32[128,96,128]{2,1,0:T(8,128)} custom-call(s32[176]{0:T(256)} %bitcast.48, s32[176]{0:T(256)} %bitcast.52, s32[3]{0:T(128)} %pad_add_fusion.info_ref, f32[64,96,128]{2,1,0:T(8,128)} %get-tuple-element.11.x_ref, f32[176,128,128]{2,1,0:T(8,128)} %bitcast.44, f32[64,96,128]{2,1,0:T(8,128)} %get-tuple-element.12.rest_0_), custom_call_target="tpu_custom_call" | custom-call | tf_op jit(solution)/shard_map/products/pallas_call | solution.py:528
  402.8 0.0 copy-start.1
  402.8 34.0 %scatter.3 = f32[16,96,128]{2,1,0:T(8,128)} custom-call(f32[128,96,128]{2,1,0:T(8,128)} %products.7.g_ref), custom_call_target="tpu_custom_call" | custom-call | tf_op jit(solution)/shard_map/scatter/pallas_call | solution.py:164
  436.8 0.0 copy-done.1
  436.8 2.2 copy_bitcast_fusion
Async XLA Ops:
  0.0 2.7 copy-start
  402.8 34.0 %copy-start.1 = (f32[16,96,128]{2,1,0:T(8,128)S(1)}, f32[16,96,128]{2,1,0:T(8,128)}, u32[]{:S(2)}) copy-start(f32[16,96,128]{2,1,0:T(8,128)} %scatter.2) | copy-start | bytes 2359300

commit v4 on v3

--- a/solution.py
+++ b/solution.py
@@ -10,6 +10,7 @@
 BS = 128
 VMEM_BYTES = 56 * 1024 * 1024
 MESH = pl.DeviceIdType.MESH
+LAG = 4
 
 
 def parts_of(total, most):
@@ -367,7 +368,7 @@
         for j in range(chunks):
             sum_up(f_ref, j).start()
 
-    lag = jnp.where(above, cols - 2 - c, c - 1) * 2
+    lag = jnp.where(above, cols - 2 - c, c - 1) * LAG
 
     def pass_on(t, carry):
         j = t - lag
@@ -402,7 +403,7 @@
 
     @pl.when(jnp.logical_not(is_root))
     def _():
-        lax.fori_loop(0, chunks + 2 * max(cols - 3, 0), pass_on, 0)
+        lax.fori_loop(0, chunks + LAG * max(cols - 3, 0), pass_on, 0)
 
     def take_in(j, carry):
         sum_ref[at(j)] = f_ref[at(j)]

time: 435 us -> 404 us (0.929); the launches traced: 439 us -> 401 us
  Pallas kernels: 431 us -> 393 us
    pallas_call x2, Pallas kernels: 235 us -> 182 us  [chain(): pl.pallas_call(functools.partial(chain_kernel, cols, ratio, chunks), out_...]
    pallas_call x2, Pallas kernels: 68 us -> 77.3 us  [scatter(): pl.pallas_call(kernel, out_shape=jax.ShapeDtypeStruct((size,) + tail, jnp...]
    pallas_call x4, Pallas kernels: 52 us -> 57.7 us  [products(): pl.pallas_call(functools.partial(products_kernel, group, contract), out_s...]
where the time goes in v4:
time: 404 us; the launch traced here: 401 us
  Pallas kernels  393 us (97%)
  other arithmetic  5 us (1%)
    pallas_call x2, Pallas kernels, chain(): pl.pallas_call(functools.partial(chain_kernel, cols, ratio, chunks), out_...  182 us
    pallas_call x2, Pallas kernels, scatter(): pl.pallas_call(kernel, out_shape=jax.ShapeDtypeStruct((size,) + tail, jnp...  77.3 us
    pallas_call x2, Pallas kernels, gather(): pl.pallas_call(kernel, out_shape=jax.ShapeDtypeStruct((rows * size,) + x....  76 us
    pallas_call x4, Pallas kernels, products(): pl.pallas_call(functools.partial(products_kernel, group, contract), out_s...  57.7 us

profile of v4, /device:TPU:0, one launch (start us, length us, event | category | flops | bytes accessed | tf_op | source)
XLA Modules:
  0.0 401.0 jit_solution(347546922566670360)
XLA Ops:
  0.0 0.0 copy-start
  2.0 0.7 pad_add_fusion.info_ref
  2.7 0.0 copy-done
  2.7 1.0 bitcast_bitcast_fusion.x_ref
  3.6 38.8 %gather.2.x_ref = f32[128,96,128]{2,1,0:T(8,128)} custom-call(f32[16,96,128]{2,1,0:T(8,128)} %bitcast_bitcast_fusion.x_ref), custom_call_target="tpu_custom_call" | custom-call | tf_op jit(solution)/shard_map/gather/pallas_call | solution.py:87
  42.4 14.2 %products.4.f_ref = f32[64,96,128]{2,1,0:T(8,128)} custom-call(s32[176]{0:T(256)} %bitcast.49, s32[176]{0:T(256)} %bitcast.45, s32[3]{0:T(128)} %pad_add_fusion.info_ref, f32[128,96,128]{2,1,0:T(8,128)} %gather.2.x_ref, f32[176,128,128]{2,1,0:T(8,128)} %bitcast.41), custom_call_target="tpu_custom_call" | custom-call | tf_op jit(solution)/shard_map/products/pallas_call | solution.py:529
  56.7 94.3 %chain.2 = (f32[64,96,128]{2,1,0:T(8,128)}, f32[64,96,128]{2,1,0:T(8,128)}) custom-call(f32[128,96,128]{2,1,0:T(8,128)} %gather.2.x_ref, f32[64,96,128]{2,1,0:T(8,128)} %products.4.f_ref), custom_call_target="tpu_custom_call" | custom-call | tf_op jit(solution)/shard_map/chain/pallas_call | solution.py:453
  151.0 14.6 %products.5.g_ref = f32[128,96,128]{2,1,0:T(8,128)} custom-call(s32[176]{0:T(256)} %bitcast.46, s32[176]{0:T(256)} %bitcast.50, s32[3]{0:T(128)} %pad_add_fusion.info_ref, f32[64,96,128]{2,1,0:T(8,128)} %get-tuple-element.9.x_ref, f32[176,128,128]{2,1,0:T(8,128)} %bitcast.42, f32[64,96,128]{2,1,0:T(8,128)} %get-tuple-element.10.rest_0_), custom_call_target="tpu_custom_call" | custom-call | tf_op jit(solution)/shard_map/products/pallas_call | solution.py:529
  165.6 37.1 %scatter.2 = f32[16,96,128]{2,1,0:T(8,128)} custom-call(f32[128,96,128]{2,1,0:T(8,128)} %products.5.g_ref), custom_call_target="tpu_custom_call" | custom-call | tf_op jit(solution)/shard_map/scatter/pallas_call | solution.py:165
  202.6 2.1 subtract_divide_fusion.x_ref
  204.8 37.2 %gather.3.x_ref = f32[128,96,128]{2,1,0:T(8,128)} custom-call(f32[16,96,128]{2,1,0:T(8,128)} %subtract_divide_fusion.x_ref), custom_call_target="tpu_custom_call" | custom-call | tf_op jit(solution)/shard_map/gather/pallas_call | solution.py:87
  242.0 14.2 %products.6.f_ref = f32[64,96,128]{2,1,0:T(8,128)} custom-call(s32[176]{0:T(256)} %bitcast.51, s32[176]{0:T(256)} %bitcast.47, s32[3]{0:T(128)} %pad_add_fusion.info_ref, f32[128,96,128]{2,1,0:T(8,128)} %gather.3.x_ref, f32[176,128,128]{2,1,0:T(8,128)} %bitcast.43), custom_call_target="tpu_custom_call" | custom-call | tf_op jit(solution)/shard_map/products/pallas_call | solution.py:529
  256.2 87.8 %chain.3 = (f32[64,96,128]{2,1,0:T(8,128)}, f32[64,96,128]{2,1,0:T(8,128)}) custom-call(f32[128,96,128]{2,1,0:T(8,128)} %gather.3.x_ref, f32[64,96,128]{2,1,0:T(8,128)} %products.6.f_ref), custom_call_target="tpu_custom_call" | custom-call | tf_op jit(solution)/shard_map/chain/pallas_call | solution.py:453
  344.0 14.6 %products.7.g_ref = f32[128,96,128]{2,1,0:T(8,128)} custom-call(s32[176]{0:T(256)} %bitcast.48, s32[176]{0:T(256)} %bitcast.52, s32[3]{0:T(128)} %pad_add_fusion.info_ref, f32[64,96,128]{2,1,0:T(8,128)} %get-tuple-element.11.x_ref, f32[176,128,128]{2,1,0:T(8,128)} %bitcast.44, f32[64,96,128]{2,1,0:T(8,128)} %get-tuple-element.12.rest_0_), custom_call_target="tpu_custom_call" | custom-call | tf_op jit(solution)/shard_map/products/pallas_call | solution.py:529
  358.6 0.0 copy-start.1
  358.6 40.2 %scatter.3 = f32[16,96,128]{2,1,0:T(8,128)} custom-call(f32[128,96,128]{2,1,0:T(8,128)} %products.7.g_ref), custom_call_target="tpu_custom_call" | custom-call | tf_op jit(solution)/shard_map/scatter/pallas_call | solution.py:165
  398.8 0.0 copy-done.1
  398.8 2.2 copy_bitcast_fusion
Async XLA Ops:
  0.0 2.7 copy-start
  358.6 40.2 %copy-start.1 = (f32[16,96,128]{2,1,0:T(8,128)S(1)}, f32[16,96,128]{2,1,0:T(8,128)}, u32[]{:S(2)}) copy-start(f32[16,96,128]{2,1,0:T(8,128)} %scatter.2) | copy-start | bytes 2359300
